TPU v7x, 32 devices: a whole 2x2x4 slice. The times are simulated.
32 devices in a mesh: basis: 8 (over y, x, core), ex: 4 (over z).
Axes of the slice: x: 2, y: 2, z: 4, core: 2. Of those that a mesh axis runs over, the one named last changes fastest.
Arguments:
- grad_out: bfloat16 [768, 13824], P('ex', 'basis'), may hold values from -6 to 6
- acts: bfloat16 [768, 5120], P('basis', 'ex'), may hold values from -6 to 6
- basis_out: bfloat16 [13824, 13824], P('basis', 'ex'), may hold values from -0.0546875 to 0.0546875
- basis_in: bfloat16 [5120, 5120], P('ex', 'basis'), may hold values from -0.078125 to 0.078125
- eigvals: float32 [13824, 5120], P('ex', 'basis'), may hold values from 0.1 to 10
- counts: int32 [48], replicated, may hold values from 1 to 16, as said below
Outputs:
- scores: float32 [16, 32], replicated
Inputs may be any that keep to these rules, and one draw needn't show every extreme that they name: `counts`: every draw holds some example with exactly 16 tokens in use.
All inputs are finite; a program needn't handle non-finite values.
Results may differ from a plain program's by a relative error of at most 0.0055.
Values may be sent and summed in bfloat16 or wider, within the bound.
A program may use at most 128 MiB of HBM per device.

v0:
```python
import jax
import jax.numpy as jnp
from jax import lax
from jax.sharding import PartitionSpec as P

D = 5120
FF = 13824
NQ = 16
NT = 32
TOKX = 16
NTOK = 768


def body(grad_out, acts, basis_out, basis_in, eigvals, counts):
    total = NTOK
    partial_grad = jnp.dot(
        lax.all_gather(grad_out, "ex", axis=0, tiled=True),
        basis_out,
        preferred_element_type=jnp.float32,
    )
    partial_act = jnp.dot(
        lax.all_gather(acts, "basis", axis=0, tiled=True),
        basis_in,
        preferred_element_type=jnp.float32,
    )
    slots = jnp.arange(total, dtype=jnp.int32)
    mask = (slots % TOKX < jnp.repeat(counts, TOKX)).astype(jnp.float32)
    summed_grad = lax.psum(partial_grad, "basis")
    rot_grad = (summed_grad * mask[:, None]).astype(jnp.bfloat16)
    rot_act = lax.psum(partial_act, "ex").astype(jnp.bfloat16)
    cols_grad = rot_grad.shape[1]
    cols_act = rot_act.shape[1]
    query_grad = rot_grad[: NQ * TOKX].reshape(NQ, TOKX, cols_grad)
    query_act = rot_act[: NQ * TOKX].reshape(NQ, TOKX, cols_act)
    train_grad = rot_grad[NQ * TOKX :]
    train_act = rot_act[NQ * TOKX :]

    def one_query(pair):
        grad_q, act_q = pair
        outer = lax.dot_general(
            grad_q, act_q, (((0,), (0,)), ((), ())), preferred_element_type=jnp.float32
        )
        precond = (outer / eigvals).astype(jnp.bfloat16)
        projected = lax.dot_general(
            train_act, precond, (((1,), (1,)), ((), ())), preferred_element_type=jnp.float32
        )
        return jnp.sum((projected * train_grad).reshape(NT, TOKX * cols_grad), axis=1)

    raw = lax.map(one_query, (query_grad, query_act))
    scaled = raw / (TOKX * jnp.sqrt(jnp.float32(FF) * jnp.float32(D)))
    return lax.psum(scaled, ("basis", "ex"))


def solution(mesh):
    return jax.shard_map(
        body,
        mesh=mesh,
        in_specs=(
            P("ex", "basis"),
            P("basis", "ex"),
            P("basis", "ex"),
            P("ex", "basis"),
            P("ex", "basis"),
            P(),
        ),
        out_specs=P(),
        check_vma=False,
    )
```

profile of v0, /device:TPU:0, one launch (start us, length us, event | category | flops | bytes accessed | tf_op | source)
XLA Modules:
  0.0 454.9 jit_solution(795550543716167153)
XLA Ops:
  8.1 60.6 %all-gather.3.cloned.1.call-done = bf16[768,1728]{1,0:T(8,128)(2,1)} async-done(((bf16[192,1728]{1,0:T(8,128)(2,1)}), bf16[768,1728]{1,0:T(8,128)(2,1)}) %all-gather.3.cloned.1.call-update) | async-done | bytes 2654224 | tf_op jit(solution)/shard_map/all_gather | solution.py:17
  68.7 16.2 %fusion.16 = f32[768,3456]{1,0:T(8,128)} fusion(bf16[768,1728]{1,0:T(8,128)(2,1)} %all-gather.3.cloned.1.call-done, bf16[1728,3456]{1,0:T(8,128)(2,1)} %param.10), kind=kOutput, calls=%fused_computation.17 | convolution fusion | flops 9172942848 | bytes 25214976 | tf_op jit(solution)/shard_map/dot_general | solution.py:16
  85.7 11.0 %all-gather.5.cloned.1.call-done = bf16[768,1280]{1,0:T(8,128)(2,1)} async-done(((bf16[96,1280]{1,0:T(8,128)(2,1)}), bf16[768,1280]{1,0:T(8,128)(2,1)}) %all-gather.5.cloned.1.call-update) | async-done | bytes 1966096 | tf_op jit(solution)/shard_map/all_gather | solution.py:22
  101.2 74.4 %all-reduce.4 = bf16[768,640]{1,0:T(8,128)(2,1)S(1)} all-reduce(f32[768,640]{1,0:T(8,128)} %fusion.17), channel_id=1, replica_groups=mesh['basis'=8,'ex'=4] {'ex'}, use_global_device_ids=true, to_apply=%region_1.2 | all-reduce | flops 491520 | bytes 2949120 | tf_op jit(solution)/shard_map/psum | solution.py:30
  176.4 74.5 %all-reduce.3.cloned.1.call-done = f32[768,3456]{1,0:T(8,128)} async-done(((f32[768,3456]{1,0:T(8,128)}), f32[768,3456]{1,0:T(8,128)}) %all-reduce.3.cloned.1.call-update) | async-done | bytes 10616848 | tf_op jit(solution)/shard_map/psum | solution.py:28
  259.5 5.9 %copy.8 = bf16[512,3456]{0,1:T(8,128)(2,1)} copy(bf16[512,3456]{1,0:T(8,128)(2,1)} %slice.19) | data formatting | bytes 7077888 | tf_op jit(solution)/shard_map/while | solution.py:49
  265.5 143.4 %while.10 = (s32[]{:T(128)}, f32[16,32]{1,0:T(8,128)S(1)}, bf16[16,16,3456]{2,1,0:T(8,128)(2,1)S(1)}, bf16[16,16,640]{2,1,0:T(8,128)(2,1)}, f32[3456,640]{1,0:T(...) while((s32[]{:T(128)}, f32[16,32]{1,0:T(8,128)S(1)}, ...), condition=%wide.region_5.6_spmd, body=%wide.region_2.5_spmd.sunk | while | flops 2345435136 | bytes 13182445 | solution.py:49
  265.5 8.7 %fusion.30 = f32[512]{0:T(512)S(1)} fusion(bf16[512,3456]{0,1:T(8,128)(2,1)} %get-tuple-element.140, bf16[512,640]{1,0:T(8,128)(2,1)S(1)} %get-tuple-element.139, f32[3456,640]{1,0:T(8,128)} %get-tuple-element.138, bf16[16,16,3456]{2,1,0:T(8,128)(2,1)S(1)} %get-tuple-element.136, s32[]{:T(128)} %get-tuple-element.124, ...), kind=kOutput, calls=%fused_computation.2.clone.1 | convolution fusion | flops 2345434624 | bytes 13175808 | tf_op jit(solution)/shard_map/while/body/eval_jaxpr/dot_general | solution.py:44
  274.4 8.7 %fusion.30 = f32[512]{0:T(512)S(1)} fusion(bf16[512,3456]{0,1:T(8,128)(2,1)} %get-tuple-element.140, bf16[512,640]{1,0:T(8,128)(2,1)S(1)} %get-tuple-element.139, f32[3456,640]{1,0:T(8,128)} %get-tuple-element.138, bf16[16,16,3456]{2,1,0:T(8,128)(2,1)S(1)} %get-tuple-element.136, s32[]{:T(128)} %get-tuple-element.124, ...), kind=kOutput, calls=%fused_computation.2.clone.1 | convolution fusion | flops 2345434624 | bytes 13175808 | tf_op jit(solution)/shard_map/while/body/eval_jaxpr/dot_general | solution.py:44
  283.4 8.7 %fusion.30 = f32[512]{0:T(512)S(1)} fusion(bf16[512,3456]{0,1:T(8,128)(2,1)} %get-tuple-element.140, bf16[512,640]{1,0:T(8,128)(2,1)S(1)} %get-tuple-element.139, f32[3456,640]{1,0:T(8,128)} %get-tuple-element.138, bf16[16,16,3456]{2,1,0:T(8,128)(2,1)S(1)} %get-tuple-element.136, s32[]{:T(128)} %get-tuple-element.124, ...), kind=kOutput, calls=%fused_computation.2.clone.1 | convolution fusion | flops 2345434624 | bytes 13175808 | tf_op jit(solution)/shard_map/while/body/eval_jaxpr/dot_general | solution.py:44
  292.4 8.7 %fusion.30 = f32[512]{0:T(512)S(1)} fusion(bf16[512,3456]{0,1:T(8,128)(2,1)} %get-tuple-element.140, bf16[512,640]{1,0:T(8,128)(2,1)S(1)} %get-tuple-element.139, f32[3456,640]{1,0:T(8,128)} %get-tuple-element.138, bf16[16,16,3456]{2,1,0:T(8,128)(2,1)S(1)} %get-tuple-element.136, s32[]{:T(128)} %get-tuple-element.124, ...), kind=kOutput, calls=%fused_computation.2.clone.1 | convolution fusion | flops 2345434624 | bytes 13175808 | tf_op jit(solution)/shard_map/while/body/eval_jaxpr/dot_general | solution.py:44
  301.3 8.7 %fusion.30 = f32[512]{0:T(512)S(1)} fusion(bf16[512,3456]{0,1:T(8,128)(2,1)} %get-tuple-element.140, bf16[512,640]{1,0:T(8,128)(2,1)S(1)} %get-tuple-element.139, f32[3456,640]{1,0:T(8,128)} %get-tuple-element.138, bf16[16,16,3456]{2,1,0:T(8,128)(2,1)S(1)} %get-tuple-element.136, s32[]{:T(128)} %get-tuple-element.124, ...), kind=kOutput, calls=%fused_computation.2.clone.1 | convolution fusion | flops 2345434624 | bytes 13175808 | tf_op jit(solution)/shard_map/while/body/eval_jaxpr/dot_general | solution.py:44
  310.3 8.7 %fusion.30 = f32[512]{0:T(512)S(1)} fusion(bf16[512,3456]{0,1:T(8,128)(2,1)} %get-tuple-element.140, bf16[512,640]{1,0:T(8,128)(2,1)S(1)} %get-tuple-element.139, f32[3456,640]{1,0:T(8,128)} %get-tuple-element.138, bf16[16,16,3456]{2,1,0:T(8,128)(2,1)S(1)} %get-tuple-element.136, s32[]{:T(128)} %get-tuple-element.124, ...), kind=kOutput, calls=%fused_computation.2.clone.1 | convolution fusion | flops 2345434624 | bytes 13175808 | tf_op jit(solution)/shard_map/while/body/eval_jaxpr/dot_general | solution.py:44
  319.2 8.7 %fusion.30 = f32[512]{0:T(512)S(1)} fusion(bf16[512,3456]{0,1:T(8,128)(2,1)} %get-tuple-element.140, bf16[512,640]{1,0:T(8,128)(2,1)S(1)} %get-tuple-element.139, f32[3456,640]{1,0:T(8,128)} %get-tuple-element.138, bf16[16,16,3456]{2,1,0:T(8,128)(2,1)S(1)} %get-tuple-element.136, s32[]{:T(128)} %get-tuple-element.124, ...), kind=kOutput, calls=%fused_computation.2.clone.1 | convolution fusion | flops 2345434624 | bytes 13175808 | tf_op jit(solution)/shard_map/while/body/eval_jaxpr/dot_general | solution.py:44
  328.2 8.7 %fusion.30 = f32[512]{0:T(512)S(1)} fusion(bf16[512,3456]{0,1:T(8,128)(2,1)} %get-tuple-element.140, bf16[512,640]{1,0:T(8,128)(2,1)S(1)} %get-tuple-element.139, f32[3456,640]{1,0:T(8,128)} %get-tuple-element.138, bf16[16,16,3456]{2,1,0:T(8,128)(2,1)S(1)} %get-tuple-element.136, s32[]{:T(128)} %get-tuple-element.124, ...), kind=kOutput, calls=%fused_computation.2.clone.1 | convolution fusion | flops 2345434624 | bytes 13175808 | tf_op jit(solution)/shard_map/while/body/eval_jaxpr/dot_general | solution.py:44
  337.2 8.7 %fusion.30 = f32[512]{0:T(512)S(1)} fusion(bf16[512,3456]{0,1:T(8,128)(2,1)} %get-tuple-element.140, bf16[512,640]{1,0:T(8,128)(2,1)S(1)} %get-tuple-element.139, f32[3456,640]{1,0:T(8,128)} %get-tuple-element.138, bf16[16,16,3456]{2,1,0:T(8,128)(2,1)S(1)} %get-tuple-element.136, s32[]{:T(128)} %get-tuple-element.124, ...), kind=kOutput, calls=%fused_computation.2.clone.1 | convolution fusion | flops 2345434624 | bytes 13175808 | tf_op jit(solution)/shard_map/while/body/eval_jaxpr/dot_general | solution.py:44
  346.1 8.7 %fusion.30 = f32[512]{0:T(512)S(1)} fusion(bf16[512,3456]{0,1:T(8,128)(2,1)} %get-tuple-element.140, bf16[512,640]{1,0:T(8,128)(2,1)S(1)} %get-tuple-element.139, f32[3456,640]{1,0:T(8,128)} %get-tuple-element.138, bf16[16,16,3456]{2,1,0:T(8,128)(2,1)S(1)} %get-tuple-element.136, s32[]{:T(128)} %get-tuple-element.124, ...), kind=kOutput, calls=%fused_computation.2.clone.1 | convolution fusion | flops 2345434624 | bytes 13175808 | tf_op jit(solution)/shard_map/while/body/eval_jaxpr/dot_general | solution.py:44
  355.1 8.7 %fusion.30 = f32[512]{0:T(512)S(1)} fusion(bf16[512,3456]{0,1:T(8,128)(2,1)} %get-tuple-element.140, bf16[512,640]{1,0:T(8,128)(2,1)S(1)} %get-tuple-element.139, f32[3456,640]{1,0:T(8,128)} %get-tuple-element.138, bf16[16,16,3456]{2,1,0:T(8,128)(2,1)S(1)} %get-tuple-element.136, s32[]{:T(128)} %get-tuple-element.124, ...), kind=kOutput, calls=%fused_computation.2.clone.1 | convolution fusion | flops 2345434624 | bytes 13175808 | tf_op jit(solution)/shard_map/while/body/eval_jaxpr/dot_general | solution.py:44
  364.0 8.7 %fusion.30 = f32[512]{0:T(512)S(1)} fusion(bf16[512,3456]{0,1:T(8,128)(2,1)} %get-tuple-element.140, bf16[512,640]{1,0:T(8,128)(2,1)S(1)} %get-tuple-element.139, f32[3456,640]{1,0:T(8,128)} %get-tuple-element.138, bf16[16,16,3456]{2,1,0:T(8,128)(2,1)S(1)} %get-tuple-element.136, s32[]{:T(128)} %get-tuple-element.124, ...), kind=kOutput, calls=%fused_computation.2.clone.1 | convolution fusion | flops 2345434624 | bytes 13175808 | tf_op jit(solution)/shard_map/while/body/eval_jaxpr/dot_general | solution.py:44
  373.0 8.7 %fusion.30 = f32[512]{0:T(512)S(1)} fusion(bf16[512,3456]{0,1:T(8,128)(2,1)} %get-tuple-element.140, bf16[512,640]{1,0:T(8,128)(2,1)S(1)} %get-tuple-element.139, f32[3456,640]{1,0:T(8,128)} %get-tuple-element.138, bf16[16,16,3456]{2,1,0:T(8,128)(2,1)S(1)} %get-tuple-element.136, s32[]{:T(128)} %get-tuple-element.124, ...), kind=kOutput, calls=%fused_computation.2.clone.1 | convolution fusion | flops 2345434624 | bytes 13175808 | tf_op jit(solution)/shard_map/while/body/eval_jaxpr/dot_general | solution.py:44
  382.0 8.7 %fusion.30 = f32[512]{0:T(512)S(1)} fusion(bf16[512,3456]{0,1:T(8,128)(2,1)} %get-tuple-element.140, bf16[512,640]{1,0:T(8,128)(2,1)S(1)} %get-tuple-element.139, f32[3456,640]{1,0:T(8,128)} %get-tuple-element.138, bf16[16,16,3456]{2,1,0:T(8,128)(2,1)S(1)} %get-tuple-element.136, s32[]{:T(128)} %get-tuple-element.124, ...), kind=kOutput, calls=%fused_computation.2.clone.1 | convolution fusion | flops 2345434624 | bytes 13175808 | tf_op jit(solution)/shard_map/while/body/eval_jaxpr/dot_general | solution.py:44
  390.9 8.7 %fusion.30 = f32[512]{0:T(512)S(1)} fusion(bf16[512,3456]{0,1:T(8,128)(2,1)} %get-tuple-element.140, bf16[512,640]{1,0:T(8,128)(2,1)S(1)} %get-tuple-element.139, f32[3456,640]{1,0:T(8,128)} %get-tuple-element.138, bf16[16,16,3456]{2,1,0:T(8,128)(2,1)S(1)} %get-tuple-element.136, s32[]{:T(128)} %get-tuple-element.124, ...), kind=kOutput, calls=%fused_computation.2.clone.1 | convolution fusion | flops 2345434624 | bytes 13175808 | tf_op jit(solution)/shard_map/while/body/eval_jaxpr/dot_general | solution.py:44
  399.9 8.7 %fusion.30 = f32[512]{0:T(512)S(1)} fusion(bf16[512,3456]{0,1:T(8,128)(2,1)} %get-tuple-element.140, bf16[512,640]{1,0:T(8,128)(2,1)S(1)} %get-tuple-element.139, f32[3456,640]{1,0:T(8,128)} %get-tuple-element.138, bf16[16,16,3456]{2,1,0:T(8,128)(2,1)S(1)} %get-tuple-element.136, s32[]{:T(128)} %get-tuple-element.124, ...), kind=kOutput, calls=%fused_computation.2.clone.1 | convolution fusion | flops 2345434624 | bytes 13175808 | tf_op jit(solution)/shard_map/while/body/eval_jaxpr/dot_general | solution.py:44
  408.9 39.5 %psum.23 = f32[16,32]{1,0:T(8,128)} all-reduce(f32[16,32]{1,0:T(8,128)S(1)} %broadcast_multiply_fusion), channel_id=1, replica_groups=mesh['basis'=8,'ex'=4] {'basis','ex'}, use_global_device_ids=true, to_apply=%region_6.7 | all-reduce | flops 512 | bytes 4096 | tf_op jit(solution)/shard_map/psum | solution.py:51
  (74 shorter events, 19.9 us)
Async XLA Ops:
  6.5 90.1 %copy-start = (bf16[1280,640]{1,0:T(8,128)(2,1)S(1)}, bf16[1280,640]{1,0:T(8,128)(2,1)}, u32[]{:S(2)}) copy-start(bf16[1280,640]{1,0:T(8,128)(2,1)} %param.11) | copy-start | bytes 4915204
  6.5 62.1 %all-gather.3.cloned.1.call-start = ((), (), s32[]{:S(2)}) async-start(), calls=%async_computation | async-start | bytes 3440640 | tf_op jit(solution)/shard_map/all_gather | solution.py:17
  7.3 89.4 %all-gather.5.cloned.1.call-start = ((), (), s32[]{:S(2)}) async-start(), calls=%async_computation.2 | async-start | bytes 2211840 | tf_op jit(solution)/shard_map/all_gather | solution.py:22
  8.0 243.0 %all-reduce.3.cloned.1.call-start = ((), (), s32[]{:S(2)}) async-start(), calls=%async_computation.1 | async-start | bytes 21233664 | tf_op jit(solution)/shard_map/psum | solution.py:28
  84.9 0.7 copy-start.3
  256.1 3.4 copy-start.2
  259.5 5.9 %slice-start = ((bf16[768,3456]{1,0:T(8,128)(2,1)}), bf16[256,3456]{1,0:T(8,128)(2,1)S(1)}, s32[]{:S(2)}) async-start(bf16[768,3456]{1,0:T(8,128)(2,1)} %copy-done.2), calls=%async_computation.3 | async-start | bytes 3538944 | tf_op jit(solution)/shard_map/slice | solution.py:33
  408.8 39.5 %copy-start.1 = (bf16[1280,640]{1,0:T(8,128)(2,1)S(1)}, bf16[1280,640]{1,0:T(8,128)(2,1)}, u32[]{:S(2)}) copy-start(bf16[1280,640]{1,0:T(8,128)(2,1)} %param.11) | copy-start | bytes 4915204
Sparse Core Ops, SparseCore 0:
  8.9 59.6 all-gather.2
  70.5 26.0 all-gather.4
  100.1 150.7 all-reduce.2
where the time goes:
time: 455 us
  matrix products  160 us (35%)
  waiting for transfers between devices  148 us (33%)
  blocking collectives  114 us (25%)
  between operations  13.2 us (3%)
  local copies, waits for them, and re-layouts  12.8 us (3%)
  other arithmetic  7 us (2%)
    dot_general x16, matrix products, one_query(): lax.dot_general(train_act, precond, (((1,), (1,)), ((), ())), preferred_e...  139 us
    psum x1, waiting for transfers between devices, body(): summed_grad = lax.psum(partial_grad, 'basis')  74.5 us
    psum x1, blocking collectives, body(): rot_act = lax.psum(partial_act, 'ex').astype(jnp.bfloat16)  74.4 us
    all_gather x1, waiting for transfers between devices, body(): lax.all_gather(grad_out, 'ex', axis=0, tiled=True)  60.6 us
    psum x1, blocking collectives, body(): return lax.psum(scaled, ('basis', 'ex'))  39.5 us
    dot_general x1, matrix products, body(): jnp.dot(lax.all_gather(grad_out, 'ex', axis=0, tiled=True), basis_out, pr...  16.2 us
    all_gather x1, waiting for transfers between devices, body(): lax.all_gather(acts, 'basis', axis=0, tiled=True)  11 us
  transfers between devices with their start and end apart: 3, of which 3 were waited for; matrix products, arithmetic and copies ran while one was open for 5% of the time, Pallas kernels for 0%

commit v1 on v0

v1 whole, which is shorter than its diff:
```python
import functools

import jax
import jax.numpy as jnp
from jax import lax
from jax.experimental import pallas as pl
from jax.experimental.pallas import tpu as pltpu
from jax.sharding import PartitionSpec as P

D = 5120
FF = 13824
NQ = 16
NT = 32
TOKX = 16
NTOK = 768
NQROWS = NQ * TOKX
LANE = 128
TILE = 512


def score_tile(o0, size, g_ref, e_ref, out_ref, gqt, ablk, recip, prec, at):
    fi = e_ref.shape[1]
    ntrain = at.shape[0]
    recip[:size, :] = 1.0 / e_ref[pl.ds(o0, size), :]
    gq = g_ref[:NQROWS, pl.ds(o0, size)].astype(jnp.float32)
    gqt[:size, :] = gq.T.astype(jnp.bfloat16)

    def pair(j, carry):
        outer = jnp.dot(gqt[:size, :], ablk[j], preferred_element_type=jnp.float32)
        for h in range(2):
            cols = slice(h * fi, (h + 1) * fi)
            prec[:size, cols] = (outer[:, cols] * recip[:size, :]).astype(jnp.bfloat16)
        proj = jnp.dot(
            g_ref[NQROWS:, pl.ds(o0, size)], prec[:size, :], preferred_element_type=jnp.float32
        )
        for h in range(2):
            prod = proj[:, h * fi : (h + 1) * fi] * at[...]
            part = prod[:, :LANE]
            for k in range(1, fi // LANE):
                part = part + prod[:, k * LANE : (k + 1) * LANE]
            out_ref[2 * j + h] += jnp.sum(part.reshape(ntrain // TOKX, TOKX, LANE), axis=1)
        return carry

    lax.fori_loop(0, NQ // 2, pair, 0)


def score_kernel(g_ref, a_ref, e_ref, out_ref, gqt, ablk, recip, prec, at):
    fo, fi = e_ref.shape
    out_ref[...] = jnp.zeros_like(out_ref)
    qa = a_ref[:NQROWS, :].astype(jnp.float32)
    owner = lax.broadcasted_iota(jnp.int32, (NQROWS, fi), 0) // TOKX

    def mask_pair(j, carry):
        for h in range(2):
            ablk[j, :, h * fi : (h + 1) * fi] = jnp.where(owner == 2 * j + h, qa, 0.0).astype(
                jnp.bfloat16
            )
        return carry

    lax.fori_loop(0, NQ // 2, mask_pair, 0)
    at[...] = a_ref[NQROWS:, :].astype(jnp.float32)
    refs = (g_ref, e_ref, out_ref, gqt, ablk, recip, prec, at)
    whole = fo // TILE

    def step(i, carry):
        score_tile(pl.multiple_of(i * TILE, TILE), TILE, *refs)
        return carry

    lax.fori_loop(0, whole, step, 0)
    if fo % TILE:
        score_tile(whole * TILE, fo % TILE, *refs)


def local_scores(rot_grad, rot_act, eigvals):
    fo, fi = eigvals.shape
    ntrain = rot_grad.shape[0] - NQROWS
    vmem = pl.BlockSpec(memory_space=pltpu.VMEM)
    sums = pl.pallas_call(
        score_kernel,
        out_shape=jax.ShapeDtypeStruct((NQ, NT, LANE), jnp.float32),
        in_specs=[vmem] * 3,
        out_specs=vmem,
        scratch_shapes=[
            pltpu.VMEM((TILE, NQROWS), jnp.bfloat16),
            pltpu.VMEM((NQ // 2, NQROWS, 2 * fi), jnp.bfloat16),
            pltpu.VMEM((TILE, fi), jnp.float32),
            pltpu.VMEM((TILE, 2 * fi), jnp.bfloat16),
            pltpu.VMEM((ntrain, fi), jnp.float32),
        ],
        compiler_params=pltpu.CompilerParams(vmem_limit_bytes=56 * 1024 * 1024),
    )(rot_grad, rot_act, eigvals)
    return jnp.sum(sums, axis=-1)


def plain_scores(rot_grad, rot_act, eigvals):
    cols_grad = rot_grad.shape[1]
    cols_act = rot_act.shape[1]
    query_grad = rot_grad[:NQROWS].reshape(NQ, TOKX, cols_grad)
    query_act = rot_act[:NQROWS].reshape(NQ, TOKX, cols_act)
    train_grad = rot_grad[NQROWS:]
    train_act = rot_act[NQROWS:]

    def one_query(pair):
        grad_q, act_q = pair
        outer = lax.dot_general(
            grad_q, act_q, (((0,), (0,)), ((), ())), preferred_element_type=jnp.float32
        )
        precond = (outer / eigvals).astype(jnp.bfloat16)
        projected = lax.dot_general(
            train_act, precond, (((1,), (1,)), ((), ())), preferred_element_type=jnp.float32
        )
        return jnp.sum((projected * train_grad).reshape(NT, TOKX * cols_grad), axis=1)

    return lax.map(one_query, (query_grad, query_act))


def body(grad_out, acts, basis_out, basis_in, eigvals, counts):
    partial_grad = jnp.dot(
        lax.all_gather(grad_out, "ex", axis=0, tiled=True),
        basis_out,
        preferred_element_type=jnp.float32,
    )
    partial_act = jnp.dot(
        lax.all_gather(acts, "basis", axis=0, tiled=True),
        basis_in,
        preferred_element_type=jnp.float32,
    )
    slots = jnp.arange(NTOK, dtype=jnp.int32)
    mask = (slots % TOKX < jnp.repeat(counts, TOKX)).astype(jnp.float32)
    summed_grad = lax.psum(partial_grad, "basis")
    rot_grad = (summed_grad * mask[:, None]).astype(jnp.bfloat16)
    rot_act = lax.psum(partial_act, "ex").astype(jnp.bfloat16)
    fo, fi = eigvals.shape
    aligned = fo % LANE == 0 and fi % LANE == 0
    raw = (local_scores if aligned else plain_scores)(rot_grad, rot_act, eigvals)
    scaled = raw / (TOKX * jnp.sqrt(jnp.float32(FF) * jnp.float32(D)))
    return lax.psum(scaled, ("basis", "ex"))


def solution(mesh):
    return jax.shard_map(
        body,
        mesh=mesh,
        in_specs=(
            P("ex", "basis"),
            P("basis", "ex"),
            P("basis", "ex"),
            P("ex", "basis"),
            P("ex", "basis"),
            P(),
        ),
        out_specs=P(),
        check_vma=False,
    )
```

time: 455 us -> 383 us (0.84)
  matrix products: 160 us -> 20.7 us
  Pallas kernels: 0 us -> 77.1 us
  local copies, waits for them, and re-layouts: 12.8 us -> 0.79 us
    dot_general x16 -> x0, matrix products: 139 us -> none  [one_query(): lax.dot_general(train_act, precond, (((1,), (1,)), ((), ())), preferred_e...]
    pallas_call x0 -> x1, Pallas kernels: none -> 77.1 us  [local_scores(): pl.pallas_call(score_kernel, out_shape=jax.ShapeDtypeStruct((NQ, NT, LANE...]
    while x1 -> x0, local copies, waits for them, and re-layouts: 5.93 us -> none  [body(): raw = lax.map(one_query, (query_grad, query_act))]
where the time goes in v1:
time: 383 us
  waiting for transfers between devices  148 us (39%)
  blocking collectives  114 us (30%)
  Pallas kernels  77.1 us (20%)
  matrix products  20.7 us (5%)
  between operations  13.1 us (3%)
  other arithmetic  8.63 us (2%)
    pallas_call x1, Pallas kernels, local_scores(): pl.pallas_call(score_kernel, out_shape=jax.ShapeDtypeStruct((NQ, NT, LANE...  77.1 us
    psum x1, waiting for transfers between devices, body(): summed_grad = lax.psum(partial_grad, 'basis')  74.9 us
    psum x1, blocking collectives, body(): rot_act = lax.psum(partial_act, 'ex').astype(jnp.bfloat16)  74.8 us
    all_gather x1, waiting for transfers between devices, body(): lax.all_gather(grad_out, 'ex', axis=0, tiled=True)  60.6 us
    psum x1, blocking collectives, body(): return lax.psum(scaled, ('basis', 'ex'))  39.5 us
    dot_general x1, matrix products, body(): jnp.dot(lax.all_gather(grad_out, 'ex', axis=0, tiled=True), basis_out, pr...  16.2 us
    all_gather x1, waiting for transfers between devices, body(): lax.all_gather(acts, 'basis', axis=0, tiled=True)  11 us
  transfers between devices with their start and end apart: 3, of which 3 were waited for; matrix products, arithmetic and copies ran while one was open for 5% of the time, Pallas kernels for 0%

profile of v1, /device:TPU:0, one launch (start us, length us, event | category | flops | bytes accessed | tf_op | source)
XLA Modules:
  0.0 382.7 jit_solution(2867561186884389314)
XLA Ops:
  6.5 0.0 copy-start
  6.5 0.0 all-gather.3.cloned.1.call-start
  6.5 0.7 all-gather.3.cloned.1.call-update
  7.3 0.0 all-gather.5.cloned.1.call-start
  7.3 0.7 all-gather.5.cloned.1.call-update
  8.0 0.0 all-reduce.3.cloned.1.call-start
  8.1 60.6 %all-gather.3.cloned.1.call-done = bf16[768,1728]{1,0:T(8,128)(2,1)} async-done(((bf16[192,1728]{1,0:T(8,128)(2,1)}), bf16[768,1728]{1,0:T(8,128)(2,1)}) %all-gather.3.cloned.1.call-update) | async-done | bytes 2654224 | tf_op jit(solution)/shard_map/all_gather | solution.py:119
  68.7 16.2 %fusion.5 = f32[768,3456]{1,0:T(8,128)} fusion(bf16[768,1728]{1,0:T(8,128)(2,1)} %all-gather.3.cloned.1.call-done, bf16[1728,3456]{1,0:T(8,128)(2,1)} %param.8), kind=kOutput, calls=%fused_computation.9 | convolution fusion | flops 9172942848 | bytes 25214976 | tf_op jit(solution)/shard_map/dot_general | solution.py:118
  84.8 0.0 copy-start.1
  84.8 0.0 all-reduce.3.cloned.1.call-update
  84.8 0.6 copy-done.1
  85.5 0.1 broadcast_in_dim.4
  85.5 0.1 reshape.18
  85.6 11.0 %all-gather.5.cloned.1.call-done = bf16[768,1280]{1,0:T(8,128)(2,1)} async-done(((bf16[96,1280]{1,0:T(8,128)(2,1)}), bf16[768,1280]{1,0:T(8,128)(2,1)}) %all-gather.5.cloned.1.call-update) | async-done | bytes 1966096 | tf_op jit(solution)/shard_map/all_gather | solution.py:124
  96.6 0.0 copy-done
  96.6 4.5 %fusion.6 = f32[768,640]{1,0:T(8,128)} fusion(bf16[768,1280]{1,0:T(8,128)(2,1)} %all-gather.5.cloned.1.call-done, bf16[1280,640]{1,0:T(8,128)(2,1)S(1)} %copy-done), kind=kOutput, calls=%fused_computation.10 | convolution fusion | flops 1258291200 | bytes 5570560 | tf_op jit(solution)/shard_map/dot_general | solution.py:123
  101.2 74.8 %all-reduce.4.a_ref = bf16[768,640]{1,0:T(8,128)(2,1)} all-reduce(f32[768,640]{1,0:T(8,128)} %fusion.6), channel_id=1, replica_groups=mesh['basis'=8,'ex'=4] {'ex'}, use_global_device_ids=true, to_apply=%region_1.2 | all-reduce | flops 491520 | bytes 2949120 | tf_op jit(solution)/shard_map/psum | solution.py:132
  176.0 74.9 %all-reduce.3.cloned.1.call-done = f32[768,3456]{1,0:T(8,128)} async-done(((f32[768,3456]{1,0:T(8,128)}), f32[768,3456]{1,0:T(8,128)}) %all-reduce.3.cloned.1.call-update) | async-done | bytes 10616848 | tf_op jit(solution)/shard_map/psum | solution.py:130
  251.0 7.5 %multiply_convert_fusion.g_ref = bf16[768,3456]{1,0:T(8,128)(2,1)} fusion(f32[768,3456]{1,0:T(8,128)} %all-reduce.3.cloned.1.call-done, f32[768]{0:T(1024)S(1)} %fusion.4), kind=kLoop, calls=%fused_computation | loop fusion | flops 5308416 | bytes 15928320 | tf_op jit(solution)/shard_map/convert_element_type | solution.py:131
  258.5 77.1 %shard_map.64 = f32[16,32,128]{2,1,0:T(8,128)} custom-call(bf16[768,3456]{1,0:T(8,128)(2,1)} %multiply_convert_fusion.g_ref, bf16[768,640]{1,0:T(8,128)(2,1)} %all-reduce.4.a_ref, f32[3456,640]{1,0:T(8,128)} %e_ref.1), custom_call_target="tpu_custom_call" | custom-call | tf_op jit(solution)/shard_map/pallas_call | solution.py:78
  335.6 1.1 reduce_sum.9
  336.7 39.5 %psum.23 = f32[16,32]{1,0:T(8,128)} all-reduce(f32[16,32]{1,0:T(8,128)S(1)} %broadcast_multiply_fusion), channel_id=1, replica_groups=mesh['basis'=8,'ex'=4] {'basis','ex'}, use_global_device_ids=true, to_apply=%region_3.4 | all-reduce | flops 512 | bytes 4096 | tf_op jit(solution)/shard_map/psum | solution.py:137
  (2 shorter events, 0.0 us)
Async XLA Ops:
  6.5 90.1 %copy-start = (bf16[1280,640]{1,0:T(8,128)(2,1)S(1)}, bf16[1280,640]{1,0:T(8,128)(2,1)}, u32[]{:S(2)}) copy-start(bf16[1280,640]{1,0:T(8,128)(2,1)} %param.9) | copy-start | bytes 4915204
  6.5 62.1 %all-gather.3.cloned.1.call-start = ((), (), s32[]{:S(2)}) async-start(), calls=%async_computation | async-start | bytes 3440640 | tf_op jit(solution)/shard_map/all_gather | solution.py:119
  7.3 89.4 %all-gather.5.cloned.1.call-start = ((), (), s32[]{:S(2)}) async-start(), calls=%async_computation.2 | async-start | bytes 2211840 | tf_op jit(solution)/shard_map/all_gather | solution.py:124
  8.0 243.0 %all-reduce.3.cloned.1.call-start = ((), (), s32[]{:S(2)}) async-start(), calls=%async_computation.1 | async-start | bytes 21233664 | tf_op jit(solution)/shard_map/psum | solution.py:130
  84.8 0.7 copy-start.1
Sparse Core Ops, SparseCore 0:
  8.9 59.6 all-gather.2
  70.5 26.0 all-gather.4
  100.1 150.7 all-reduce.2

commit v2 on v1

--- a/solution.py
+++ b/solution.py
@@ -114,7 +114,321 @@
     return lax.map(one_query, (query_grad, query_act))
 
 
-def body(grad_out, acts, basis_out, basis_in, eigvals, counts):
+MESH = pl.DeviceIdType.MESH
+CHIPS = 4
+CORES = 2
+PLANE = CHIPS * CORES
+LINE = 4
+COLS = 384
+
+
+def remote(src, dst, send, recv, **where):
+    return pltpu.make_async_remote_copy(
+        src_ref=src,
+        dst_ref=dst,
+        send_sem=send,
+        recv_sem=recv,
+        device_id=where,
+        device_id_type=MESH,
+    )
+
+
+def greet(partners):
+    barrier = pltpu.get_barrier_semaphore()
+    for where in partners:
+        pl.semaphore_signal(barrier, inc=1, device_id=where, device_id_type=MESH)
+    pl.semaphore_wait(barrier, len(partners))
+
+
+def rotate_kernel(
+    g_ref, a_ref, bo_ref, bi_ref, mask_ref, grad_ref, act_ref,
+    gg, aa, part, sib, rsend, rrecv, apart, arecv,
+    zs, zr, xs, xr, fs, fr, ss, sr, rs, rr, gs, gr, hs, hr, us, ur, vs, vr,
+):
+    rows, depth = g_ref.shape
+    fo = bo_ref.shape[1]
+    quarter = rows // CHIPS
+    b = lax.axis_index("basis")
+    z = lax.axis_index("ex")
+    chip, core = b // CORES, b % CORES
+    twin = chip * CORES + 1 - core
+
+    def chip_at(k):
+        return lax.rem(chip + k + CHIPS, CHIPS)
+
+    def mate(k):
+        return chip_at(k) * CORES + core
+
+    def line_at(k):
+        return lax.rem(z + k + LINE, LINE)
+
+    near = z // 2
+    mirrored = z * (1 - near) + (LINE - 1 - z) * near
+
+    def shard_at(place):
+        m = (mirrored, 1 - mirrored, 2, 3)[place]
+        return m * (1 - near) + (LINE - 1 - m) * near
+
+    greet(
+        [{"basis": mate(k)} for k in range(1, CHIPS)]
+        + [{"basis": twin}]
+        + [{"ex": line_at(k)} for k in range(1, LINE)]
+    )
+
+    waits = []
+
+    def begin(copy):
+        copy.start()
+        waits.append(copy)
+
+    for k in (1, 3, 2):
+        begin(remote(g_ref, gg.at[z], zs.at[k], zr.at[z], ex=line_at(k)))
+    for k in (1, 2, 3):
+        begin(remote(a_ref, aa.at[b], xs.at[k], xr.at[k], basis=mate(k)))
+    begin(remote(a_ref, aa.at[b], fs.at[0], fr.at[0], basis=twin))
+    aa[b] = a_ref[...]
+
+    def multiply(place, src):
+        half, slot = place // 2, place % 2
+
+        def chunk(c, carry):
+            cols = pl.ds(pl.multiple_of(c * COLS, COLS), COLS)
+            part[half, slot, :, cols] = jnp.dot(
+                src[...], bo_ref[:, cols], preferred_element_type=jnp.float32
+            )
+            return carry
+
+        lax.fori_loop(0, fo // COLS, chunk, 0)
+
+    def arrive(place):
+        shard = shard_at(place)
+        remote(gg.at[shard], gg.at[shard], zs.at[0], zr.at[shard], ex=line_at(1)).wait_recv()
+        multiply(place, gg.at[shard])
+
+    def pair_send(half):
+        begin(
+            remote(part.at[half, 1 - core], sib.at[half], ss.at[half], sr.at[half], basis=twin)
+        )
+
+    def pair_sum(half, t):
+        at = pl.ds(pl.multiple_of(t * quarter, 16), quarter)
+        return part[half, core, at, :] + sib[half, at, :]
+
+    def scatter(half):
+        remote(sib.at[half], sib.at[half], ss.at[half], sr.at[half], basis=twin).wait_recv()
+        for k in (1, 2, 3):
+            rsend[half, k - 1] = pair_sum(half, chip_at(k)).astype(jnp.bfloat16)
+            begin(
+                remote(
+                    rsend.at[half, k - 1], rrecv.at[half, k - 1],
+                    rs.at[half, k - 1], rr.at[half, k - 1], basis=mate(k),
+                )
+            )
+
+    def block(half, c, t):
+        even, odd = shard_at(2 * half), shard_at(2 * half + 1)
+        shard = even * (1 - c) + odd * c
+        return pl.ds(pl.multiple_of(shard * rows + t * quarter, 16), quarter)
+
+    def finish(half):
+        total = pair_sum(half, chip)
+        for k in (1, 2, 3):
+            dst = rrecv.at[half, k - 1]
+            remote(dst, dst, rs.at[half, k - 1], rr.at[half, k - 1], basis=twin).wait_recv()
+            total = total + rrecv[half, k - 1].astype(jnp.float32)
+        mine = block(half, core, chip)
+        grad_ref[mine, :] = (total * mask_ref[mine, :]).astype(jnp.bfloat16)
+        own = grad_ref.at[mine, :]
+        for k in (1, 2, 3):
+            begin(remote(own, own, gs.at[half, k], gr.at[half, k], basis=mate(k)))
+        begin(remote(own, own, hs.at[half, 0], hr.at[half, 0], basis=twin))
+
+    def forward(half):
+        for k in (1, 2, 3):
+            got = grad_ref.at[block(half, core, chip_at(-k)), :]
+            remote(got, got, gs.at[half, k], gr.at[half, k], basis=twin).wait_recv()
+            begin(remote(got, got, hs.at[half, k], hr.at[half, k], basis=twin))
+
+    def settle(half):
+        for k in range(CHIPS):
+            got = grad_ref.at[block(half, 1 - core, chip_at(-k)), :]
+            remote(got, got, hs.at[half, k], hr.at[half, k], basis=twin).wait_recv()
+
+    multiply(0, g_ref)
+    for k in (1, 2, 3):
+        got = aa.at[mate(-k)]
+        remote(got, got, xs.at[k], xr.at[k], basis=twin).wait_recv()
+        begin(remote(got, got, fs.at[k], fr.at[k], basis=twin))
+    arrive(1)
+    pair_send(0)
+    for k in range(CHIPS):
+        got = aa.at[chip_at(-k) * CORES + 1 - core]
+        remote(got, got, fs.at[k], fr.at[k], basis=twin).wait_recv()
+    tokens = aa.shape[1]
+    for i in range(PLANE):
+        apart[i * tokens : (i + 1) * tokens, :] = jnp.dot(
+            aa[i], bi_ref[...], preferred_element_type=jnp.float32
+        )
+
+    def line_block(t):
+        return pl.ds(pl.multiple_of(t * rows, 16), rows)
+
+    for k in (1, 3, 2):
+        begin(
+            remote(
+                apart.at[line_block(line_at(k)), :], arecv.at[k - 1],
+                us.at[k - 1], ur.at[k - 1], ex=line_at(k),
+            )
+        )
+    scatter(0)
+    arrive(2)
+    finish(0)
+    arrive(3)
+    pair_send(1)
+    total = apart[line_block(z), :]
+    for k in (1, 2, 3):
+        dst = arecv.at[k - 1]
+        remote(dst, dst, us.at[k - 1], ur.at[k - 1], ex=line_at(1)).wait_recv()
+        total = total + arecv[k - 1]
+    act_ref[line_block(z), :] = total.astype(jnp.bfloat16)
+    own = act_ref.at[line_block(z), :]
+    scatter(1)
+    for k in (1, 3, 2):
+        begin(remote(own, own, vs.at[k - 1], vr.at[k - 1], ex=line_at(k)))
+    forward(0)
+    finish(1)
+    settle(0)
+    forward(1)
+    for k in (1, 2, 3):
+        got = act_ref.at[line_block(line_at(-k)), :]
+        remote(got, got, vs.at[k - 1], vr.at[k - 1], ex=line_at(1)).wait_recv()
+    settle(1)
+    for copy in waits:
+        copy.wait_send()
+
+
+def rotate(grad_out, acts, basis_out, basis_in, mask):
+    rows, depth = grad_out.shape
+    tokens, feats = acts.shape
+    fo, fi = basis_out.shape[1], basis_in.shape[1]
+    total = rows * LINE
+    vmem = pl.BlockSpec(memory_space=pltpu.VMEM)
+    dma = pltpu.SemaphoreType.DMA
+    f32, b16 = jnp.float32, jnp.bfloat16
+    return pl.pallas_call(
+        rotate_kernel,
+        out_shape=(
+            jax.ShapeDtypeStruct((total, fo), b16),
+            jax.ShapeDtypeStruct((total, fi), b16),
+        ),
+        in_specs=[vmem] * 5,
+        out_specs=(vmem, vmem),
+        scratch_shapes=[
+            pltpu.VMEM((LINE, rows, depth), b16),
+            pltpu.VMEM((PLANE, tokens, feats), b16),
+            pltpu.VMEM((2, 2, rows, fo), f32),
+            pltpu.VMEM((2, rows, fo), f32),
+            pltpu.VMEM((2, 3, rows // CHIPS, fo), b16),
+            pltpu.VMEM((2, 3, rows // CHIPS, fo), b16),
+            pltpu.VMEM((total, fi), f32),
+            pltpu.VMEM((3, rows, fi), f32),
+            dma((4,)), dma((4,)),
+            dma((4,)), dma((4,)),
+            dma((4,)), dma((4,)),
+            dma((2,)), dma((2,)),
+            dma((2, 3)), dma((2, 3)),
+            dma((2, 4)), dma((2, 4)),
+            dma((2, 4)), dma((2, 4)),
+            dma((3,)), dma((3,)),
+            dma((3,)), dma((3,)),
+        ],
+        compiler_params=pltpu.CompilerParams(
+            collective_id=0, has_side_effects=True, vmem_limit_bytes=62 * 1024 * 1024
+        ),
+        cost_estimate=pl.CostEstimate(
+            flops=2 * total * depth * fo, bytes_accessed=30 * 1024 * 1024, transcendentals=0
+        ),
+    )(grad_out, acts, basis_out, basis_in, mask)
+
+
+def sum_kernel(x_ref, out_ref, plane, line, ps, pr, ls, lr):
+    b = lax.axis_index("basis")
+    z = lax.axis_index("ex")
+    greet(
+        [{"basis": lax.rem(b + k, PLANE)} for k in range(1, PLANE)]
+        + [{"ex": lax.rem(z + k, LINE)} for k in range(1, LINE)]
+    )
+    copies = []
+    plane[b] = x_ref[...]
+    for k in range(1, PLANE):
+        to = lax.rem(b + k, PLANE)
+        copies.append(remote(x_ref, plane.at[b], ps.at[k], pr.at[k], basis=to))
+        copies[-1].start()
+    for k in range(1, PLANE):
+        got = plane.at[lax.rem(b - k + PLANE, PLANE)]
+        remote(got, got, ps.at[k], pr.at[k], basis=lax.rem(b + 1, PLANE)).wait_recv()
+    total = plane[0]
+    for i in range(1, PLANE):
+        total = total + plane[i]
+    line[z] = total
+    own = line.at[z]
+    for k in range(1, LINE):
+        to = lax.rem(z + k, LINE)
+        copies.append(remote(own, own, ls.at[k], lr.at[k], ex=to))
+        copies[-1].start()
+    for k in range(1, LINE):
+        got = line.at[lax.rem(z - k + LINE, LINE)]
+        remote(got, got, ls.at[k], lr.at[k], ex=lax.rem(z + 1, LINE)).wait_recv()
+    total = line[0]
+    for i in range(1, LINE):
+        total = total + line[i]
+    out_ref[...] = total
+    for copy in copies:
+        copy.wait_send()
+
+
+def sum_all(x):
+    flat = jnp.pad(x.reshape(-1, LANE), ((0, 8 - x.size // LANE), (0, 0)))
+    vmem = pl.BlockSpec(memory_space=pltpu.VMEM)
+    dma = pltpu.SemaphoreType.DMA
+    total = pl.pallas_call(
+        sum_kernel,
+        out_shape=jax.ShapeDtypeStruct(flat.shape, flat.dtype),
+        in_specs=[vmem],
+        out_specs=vmem,
+        scratch_shapes=[
+            pltpu.VMEM((PLANE,) + flat.shape, flat.dtype),
+            pltpu.VMEM((LINE,) + flat.shape, flat.dtype),
+            dma((PLANE,)), dma((PLANE,)),
+            dma((LINE,)), dma((LINE,)),
+        ],
+        compiler_params=pltpu.CompilerParams(collective_id=1, has_side_effects=True),
+    )(flat)
+    return total[: x.size // LANE].reshape(x.shape)
+
+
+def slot_mask(counts):
+    slots = jnp.arange(NTOK, dtype=jnp.int32)
+    return (slots % TOKX < jnp.repeat(counts, TOKX)).astype(jnp.float32)[:, None]
+
+
+def fits(mesh, grad_out, acts, eigvals):
+    fo, fi = eigvals.shape
+    return (
+        mesh["basis"] == PLANE
+        and mesh["ex"] == LINE
+        and fo % COLS == 0
+        and fi % LANE == 0
+        and grad_out.shape[0] % (16 * CHIPS) == 0
+        and acts.shape[0] % 16 == 0
+    )
+
+
+def body(grad_out, acts, basis_out, basis_in, eigvals, counts, mesh):
+    scale = TOKX * jnp.sqrt(jnp.float32(FF) * jnp.float32(D))
+    if fits(mesh, grad_out, acts, eigvals):
+        rot_grad, rot_act = rotate(grad_out, acts, basis_out, basis_in, slot_mask(counts))
+        return sum_all(local_scores(rot_grad, rot_act, eigvals) / scale)
     partial_grad = jnp.dot(
         lax.all_gather(grad_out, "ex", axis=0, tiled=True),
         basis_out,
@@ -125,21 +439,16 @@
         basis_in,
         preferred_element_type=jnp.float32,
     )
-    slots = jnp.arange(NTOK, dtype=jnp.int32)
-    mask = (slots % TOKX < jnp.repeat(counts, TOKX)).astype(jnp.float32)
     summed_grad = lax.psum(partial_grad, "basis")
-    rot_grad = (summed_grad * mask[:, None]).astype(jnp.bfloat16)
+    rot_grad = (summed_grad * slot_mask(counts)).astype(jnp.bfloat16)
     rot_act = lax.psum(partial_act, "ex").astype(jnp.bfloat16)
-    fo, fi = eigvals.shape
-    aligned = fo % LANE == 0 and fi % LANE == 0
-    raw = (local_scores if aligned else plain_scores)(rot_grad, rot_act, eigvals)
-    scaled = raw / (TOKX * jnp.sqrt(jnp.float32(FF) * jnp.float32(D)))
-    return lax.psum(scaled, ("basis", "ex"))
+    raw = plain_scores(rot_grad, rot_act, eigvals)
+    return lax.psum(raw / scale, ("basis", "ex"))
 
 
 def solution(mesh):
     return jax.shard_map(
-        body,
+        functools.partial(body, mesh=dict(mesh.shape)),
         mesh=mesh,
         in_specs=(
             P("ex", "basis"),

time: 383 us -> 242 us (0.63)
  Pallas kernels: 77.1 us -> 237 us
  waiting for transfers between devices: 148 us -> 0 us
  blocking collectives: 114 us -> 0 us
  matrix products: 20.7 us -> 0 us
  between operations: 13.1 us -> 0.04 us
  other arithmetic: 8.63 us -> 1.91 us
    pallas_call x0 -> x2, Pallas kernels: none -> 160 us  [the longest x1 149 us: rotate(): pl.pallas_call(rotate_kernel, out_shape=(jax.ShapeDtypeStruct((total, fo)...]
    psum x2 -> x0, blocking collectives: 114 us -> none  [the longest x1 74.8 us: body(): rot_act = lax.psum(partial_act, 'ex').astype(jnp.bfloat16)]
    psum x1 -> x0, waiting for transfers between devices: 74.9 us -> none  [body(): summed_grad = lax.psum(partial_grad, 'basis')]
    all_gather x2 -> x0, waiting for transfers between devices: 71.6 us -> none  [the longest x1 60.6 us: body(): lax.all_gather(grad_out, 'ex', axis=0, tiled=True)]
    dot_general x2 -> x0, matrix products: 20.7 us -> none  [the longest x1 16.2 us: body(): jnp.dot(lax.all_gather(grad_out, 'ex', axis=0, tiled=True), basis_out, pr...]
    convert_element_type x2 -> x1, other arithmetic: 7.54 us -> 0.8 us  [slot_mask(): (slots % TOKX < jnp.repeat(counts, TOKX)).astype(jnp.float32)[:, None]]
  transfers between devices with their start and end apart: 3 -> 0, of which waited for: 3 -> 0; matrix products, arithmetic and copies ran while one was open for 5% -> 0% of each run, Pallas kernels for 0% -> 0%
where the time goes in v2:
time: 242 us
  Pallas kernels  237 us (98%)
  local copies, waits for them, and re-layouts  3.09 us (1%)
    pallas_call x1, Pallas kernels, rotate(): pl.pallas_call(rotate_kernel, out_shape=(jax.ShapeDtypeStruct((total, fo)...  149 us
    pallas_call x1, Pallas kernels, local_scores(): pl.pallas_call(score_kernel, out_shape=jax.ShapeDtypeStruct((NQ, NT, LANE...  77.1 us
    pallas_call x1, Pallas kernels, sum_all(): pl.pallas_call(sum_kernel, out_shape=jax.ShapeDtypeStruct(flat.shape, fla...  10.6 us

profile of v2, /device:TPU:0, one launch (start us, length us, event | category | flops | bytes accessed | tf_op | source)
XLA Modules:
  0.0 241.7 jit_solution(7597508517575796763)
XLA Ops:
  0.0 0.7 broadcast_in_dim.4
  0.7 0.1 reshape.45
  0.8 0.2 copy.8
  1.1 0.8 convert_element_type.12.mask_ref
  1.9 149.0 %shard_map.64 = (bf16[768,3456]{1,0:T(8,128)(2,1)}, bf16[768,640]{1,0:T(8,128)(2,1)}) custom-call(bf16[192,1728]{1,0:T(8,128)(2,1)} %g_ref.1, bf16[96,1280]{1,0:T(8,128)(2,1)} %a_ref.1, bf16[1728,3456]{1,0:T(8,128)(2,1)} %bo_ref.1, bf16[1280,640]{1,0:T(8,128)(2,1)} %bi_ref.1, f32[768,1]{1,0:T(8,128)} %convert_element_type.12.mask_ref), custom_call_target="tpu_custom_call" | custom-call | flops 9172942848 | bytes 31457280 | tf_op jit(solution)/shard_map/pallas_call | solution.py:318
  150.9 77.1 %shard_map.65 = f32[16,32,128]{2,1,0:T(8,128)} custom-call(bf16[768,3456]{1,0:T(8,128)(2,1)} %get-tuple-element.7.g_ref, bf16[768,640]{1,0:T(8,128)(2,1)} %get-tuple-element.8.a_ref, f32[3456,640]{1,0:T(8,128)} %e_ref.1), custom_call_target="tpu_custom_call" | custom-call | tf_op jit(solution)/shard_map/pallas_call | solution.py:78
  228.0 1.1 reduce_sum.9
  229.1 0.1 div.10
  229.2 0.6 pad.4.x_ref
  229.8 10.6 %shard_map.66 = f32[8,128]{1,0:T(8,128)} custom-call(f32[8,128]{1,0:T(8,128)} %pad.4.x_ref), custom_call_target="tpu_custom_call" | custom-call | tf_op jit(solution)/shard_map/pallas_call | solution.py:394
  240.3 0.7 slice.3
  241.0 0.7 reshape.46
  (2 shorter events, 0.0 us)
